TPU v7x, 512 devices: a whole 4x8x8 slice. The times are simulated.
512 devices in a mesh: cell: 8 (over z), donor: 8 (over x, core), gene: 8 (over y).
Axes of the slice: x: 4, y: 8, z: 8, core: 2. Of those that a mesh axis runs over, the one named last changes fastest.
Arguments:
- counts: int32 [32768, 2048], P(('cell', 'donor'), 'gene'), may hold values from 0 to 35
- cell_donor: int32 [32768], P(('cell', 'donor')), may hold values from 0 to 511, as said below
- cell_type: int32 [32768], P(('cell', 'donor')), may hold values from -1 to 23, as said below
- covariates: float32 [512, 50], P(('cell', 'donor')), may hold values from -6 to 6
- dosage: int32 [8192, 512], P('gene'), may hold values from 0 to 2
- windows: int32 [2048, 1024], P(('gene', 'cell', 'donor')), may hold values from -1 to 8191, as said below
Outputs:
- association: float32 [24, 2048, 1024], P(None, ('gene', 'cell', 'donor'))
Inputs may be any that keep to these rules, and one draw needn't show every extreme that they name: `cell_donor`: rows come in blocks of 512: a row of block b names a donor d with (d // 8) % 8 = b % 8. Every donor has at least one cell of every cell type. `cell_type`: in each block of 512 rows the live slots (type 0 or more) come first and the empty ones (-1) last; the number of live slots varies from block to block and some block is full. `windows`: row j lists consecutive SNP numbers in ascending order, then -1 to its end; all of them lie in [b * 1024, (b + 1) * 1024) with b = j // 256. A window holds 512 to 1024 SNPs, some window holds exactly 1024, and the last gene's window ends at the last SNP.
All inputs are finite; a program needn't handle non-finite values.
Results may differ from a plain program's by a relative error of at most 0.00045.
Values sent between devices are 32-bit elements; how exact they have to be, the bound alone decides.
No kernel may reach another device: no remote copies, remote signals or barrier semaphores. Data moves between devices by JAX's collectives and lax.ppermute only.
A program may use at most 64 MiB of HBM per device.

v0:
```python
import math
import jax
import jax.numpy as jnp
from jax import lax
from jax.sharding import PartitionSpec as P

CT = 24


def log_cpm(pseudobulk, library):
    return jnp.log2((pseudobulk + 0.5) / (library + 1.0) * 1000000.0)


def with_intercept(covariates):
    intercept = jnp.ones((covariates.shape[0], 1), jnp.float32)
    return jnp.concatenate([intercept, covariates], axis=1)


def factor_lower(gram_sum):
    order = gram_sum.shape[0]
    factor = jnp.zeros_like(gram_sum)
    for column in range(order):
        known = factor[column, :column]
        pivot = jnp.sqrt(gram_sum[column, column] - jnp.sum(known * known))
        factor = factor.at[column, column].set(pivot)
        if column + 1 < order:
            below = gram_sum[column + 1 :, column] - jnp.dot(
                factor[column + 1 :, :column], known, precision=lax.Precision.HIGHEST
            )
            factor = factor.at[column + 1 :, column].set(below / pivot)
    return factor


def solve_written(factor, right_rows):
    order = factor.shape[0]
    forward = []
    for row in range(order):
        value = right_rows[row]
        if row > 0:
            value = value - jnp.dot(
                factor[row, :row], jnp.stack(forward), precision=lax.Precision.HIGHEST
            )
        forward.append(value / factor[row, row])
    backward = [None] * order
    for row in range(order - 1, -1, -1):
        value = forward[row]
        if row < order - 1:
            later = jnp.stack(backward[row + 1 :])
            value = value - jnp.dot(factor[row + 1 :, row], later, precision=lax.Precision.HIGHEST)
        backward[row] = value / factor[row, row]
    return jnp.stack(backward)


def solve_normal(gram_sum, cross_sum):
    order = gram_sum.shape[0]
    factor = factor_lower(gram_sum)
    inverse = solve_written(factor, jnp.eye(order, dtype=jnp.float32))
    return jnp.einsum("kj,cjg->ckg", inverse, cross_sum, precision=lax.Precision.HIGHEST)


def association_block(residual, dosage, windows, first_snp):
    window_len = windows.shape[1]
    every_snp = jnp.einsum(
        "sd,dcg->gsc", dosage.astype(jnp.float32), residual, precision=lax.Precision.HIGHEST
    )
    padded = jnp.pad(every_snp, ((0, 0), (0, window_len), (0, 0)))
    starts = windows[:, 0] - first_snp
    gene_ids = jnp.arange(windows.shape[0], dtype=jnp.int32)

    def one_gene(pair):
        gene_id, start = pair
        gene_rows = lax.dynamic_index_in_dim(padded, gene_id, 0, keepdims=False)
        return lax.dynamic_slice_in_dim(gene_rows, start, window_len, 0)

    sliced = lax.map(one_gene, (gene_ids, starts))
    products = jnp.transpose(sliced, (2, 0, 1))
    scaling = 1.0 / math.sqrt(dosage.shape[1])
    return jnp.where((windows >= 0)[None], products, 0.0) * scaling


def owner_index(cell_donor, cell_type, donors_here, groups):
    cell_slot = cell_donor // (donors_here * groups)
    local_donor = cell_slot * donors_here + cell_donor % donors_here
    return jnp.where(cell_type >= 0, local_donor * CT + cell_type, -1)


def per_device(counts, cell_donor, cell_type, covariates, dosage, windows):
    groups = lax.axis_size("donor")
    donors_here = covariates.shape[0]
    cell_count = counts.shape[0]
    owner_slot = owner_index(cell_donor, cell_type, donors_here, groups)
    counts_half = counts.astype(jnp.bfloat16)
    first_snp = lax.axis_index("gene") * dosage.shape[0]
    row_ids = lax.broadcasted_iota(
        jnp.int32, (donors_here * CT * lax.axis_size("cell"), cell_count), 0
    )
    onehot_table = (row_ids == owner_slot[None, :]).astype(jnp.bfloat16)
    pseudobulk = lax.psum_scatter(
        jnp.dot(onehot_table, counts_half, preferred_element_type=jnp.float32),
        "cell",
        scatter_dimension=0,
        tiled=True,
    )
    library = lax.psum(jnp.sum(pseudobulk, axis=1), "gene")
    expression = log_cpm(pseudobulk, library[:, None]).reshape(donors_here, CT, -1)
    design = with_intercept(covariates)
    gram_part = jnp.dot(design.T, design, precision=lax.Precision.HIGHEST)
    cross_part = jnp.einsum("dk,dcg->ckg", design, expression, precision=lax.Precision.HIGHEST)
    gram_sum, cross_sum = lax.psum((gram_part, cross_part), ("cell", "donor"))
    coefficients = solve_normal(gram_sum, cross_sum)
    residual = expression - jnp.einsum(
        "dk,ckg->dcg", design, coefficients, precision=lax.Precision.HIGHEST
    )
    regrouped = lax.all_to_all(residual, ("cell", "donor"), split_axis=2, concat_axis=0, tiled=True)
    return association_block(regrouped, dosage, windows, first_snp)


def solution(mesh):
    in_specs = (
        P(("cell", "donor"), "gene"),
        P(("cell", "donor")),
        P(("cell", "donor")),
        P(("cell", "donor"), None),
        P("gene", None),
        P(("gene", "cell", "donor"), None),
    )
    out_specs = P(None, ("gene", "cell", "donor"), None)
    return jax.shard_map(
        per_device, mesh=mesh, in_specs=in_specs, out_specs=out_specs, check_vma=False
    )
```

profile of v0, /device:TPU:1, one launch (start us, length us, event | category | flops | bytes accessed | tf_op | source)
XLA Modules:
  0.0 813.1 jit_solution(3078640551746485459)
XLA Ops:
  7.3 2.8 fusion
  10.5 252.7 %psum.23 = f32[51,51]{1,0:T(8,128)S(1)} all-reduce(f32[51,51]{1,0:T(8,128)S(1)} %fusion.449), channel_id=1, replica_groups=mesh['cell'=8,'donor'=8,'gene'=8] {'cell','donor'}, use_global_device_ids=true, to_apply=%region_4.5 | all-reduce | flops 2601 | bytes 20808 | tf_op jit(solution)/shard_map/psum | solution.py:109
  375.8 11.7 %scatter.456 = f32[51,51]{1,0:T(8,128)S(1)} dynamic-update-slice(f32[51,51]{1,0:T(8,128)S(1)} %copy.362, f32[1,1]{1,0:T(1,128)} %bitcast.220, s32[]{:T(128)} %constant.2846.clone.1, s32[]{:T(128)} %constant.2846.clone.1) | dynamic-update-slice | bytes 12 | tf_op jit(solution)/shard_map/scatter | solution.py:25
  431.1 1.8 fusion.481
  497.7 0.8 fusion.295
  510.8 0.8 fusion.321
  517.2 1.0 reduce_sum.454
  518.2 14.1 %psum.21 = f32[192]{0:T(256)S(1)} all-reduce(f32[192]{0:T(256)S(1)} %reduce_sum.454), channel_id=1, replica_groups=mesh['cell'=8,'donor'=8,'gene'=8] {'gene'}, use_global_device_ids=true, to_apply=%region_2.3 | all-reduce | flops 192 | bytes 1536 | tf_op jit(solution)/shard_map/psum | solution.py:104
  532.3 1.0 log_multiply_fusion
  533.3 2.5 convolution_bitcast_fusion.1
  537.1 1.4 fusion.335
  539.7 193.4 %all-reduce.5.cloned.1.call-done = f32[24,51,256]{2,1,0:T(8,128)} async-done(((f32[24,51,256]{2,1,0:T(8,128)}), f32[24,51,256]{2,1,0:T(8,128)}) %all-reduce.5.cloned.1.call-update) | async-done | bytes 1253392 | tf_op jit(solution)/shard_map/psum | solution.py:109
  733.0 2.6 convolution_bitcast_fusion
  736.9 1.5 reshape.3475
  738.4 9.8 %all-to-all-start = ((f32[64,1,768]{2,1,0:T(1,128)}), f32[64,1,768]{2,1,0:T(1,128)S(1)}, u32[]{:S(2)}, u32[]{:S(2)}) async-start(f32[64,1,768]{2,1,0:T(1,128)} %reshape.3475), calls=%async_computation.1 | async-start | bytes 393216 | tf_op jit(solution)/shard_map/all_to_all | solution.py:114
  748.3 11.7 %all-to-all-done = f32[64,1,768]{2,1,0:T(1,128)S(1)} async-done(((f32[64,1,768]{2,1,0:T(1,128)}), f32[64,1,768]{2,1,0:T(1,128)S(1)}, u32[]{:S(2)}, u32[]{:S(2)}) %all-to-all-start) | async-done | bytes 196640 | tf_op jit(solution)/shard_map/all_to_all | solution.py:114
  760.6 1.2 reduce.398
  762.6 6.8 fusion.5
  769.4 34.5 %while.115 = (s32[]{:T(128)}, f32[4,1024,24]{1,0,2:T(4,128)}, s32[4]{0:T(128)S(1)}, s32[4]{0:T(128)S(1)}, f32[4,2048,24]{1,2,0:T(8,128)S(1)}) while((s32[]{:T(128)}, f32[4,1024,24]{1,0,2:T(4,128)}, s32[4]{0:T(128)S(1)}, s32[4]{0:T(128)S(1)}, f32[4,2048,24]{1,2,0:T(8,128)S(1)}) %tuple.543), condition=%wide.region_55.56_spmd.clone, body=%wide.region_54.55_spmd.sunk.clone | while | flops 10 | bytes 590021 | solution.py:75
  775.1 2.9 dynamic_update_slice.10
  783.8 2.9 dynamic_update_slice.10
  792.4 2.9 dynamic_update_slice.10
  801.0 2.9 dynamic_update_slice.10
  803.9 1.9 multiply_bitcast_fusion
  (625 shorter events, 181.2 us)
Async XLA Ops:
  6.5 510.6 %reduce-scatter.2.cloned.1.call-start = ((), (), s32[]{:S(2)}) async-start(), calls=%async_computation.2 | async-start | bytes 1769472 | tf_op jit(solution)/shard_map/reduce_scatter | solution.py:98
  7.2 2.9 copy-start.1
  10.1 722.9 %all-reduce.5.cloned.1.call-start = ((), (), s32[]{:S(2)}) async-start(), calls=%async_computation.3 | async-start | bytes 2752512 | tf_op jit(solution)/shard_map/psum | solution.py:109
  736.4 11.7 %copy-start.2 = (s32[4,1024]{1,0:T(4,128)S(1)}, s32[4,1024]{1,0:T(4,128)}, u32[]{:S(2)}) copy-start(s32[4,1024]{1,0:T(4,128)} %param.215) | copy-start | bytes 49156
  736.9 25.7 %copy-start = (s32[1024,512]{1,0:T(8,128)S(1)}, s32[1024,512]{1,0:T(8,128)}, u32[]{:S(2)}) copy-start(s32[1024,512]{1,0:T(8,128)} %param.214) | copy-start | bytes 6291460
  738.4 21.7 %all-to-all-start = ((f32[64,1,768]{2,1,0:T(1,128)}), f32[64,1,768]{2,1,0:T(1,128)S(1)}, u32[]{:S(2)}, u32[]{:S(2)}) async-start(f32[64,1,768]{2,1,0:T(1,128)} %reshape.3475), calls=%async_computation.1 | async-start | bytes 393216 | tf_op jit(solution)/shard_map/all_to_all | solution.py:114
Sparse Core Ops, SparseCore 0:
  10.3 45.2 reduce-scatter.1
  535.9 197.0 all-reduce.4
where the time goes:
time: 824 us; the launch traced here: 813 us
  blocking collectives  267 us (32%)
  waiting for transfers between devices  205 us (25%)
  matrix products  96.3 us (12%)
  local copies, waits for them, and re-layouts  94.6 us (11%)
  between operations  84 us (10%)
  other arithmetic  39.8 us (5%)
  loops' own time  16.7 us (2%)
  starting transfers between devices  9.82 us (1%)
    psum x1, blocking collectives, per_device(): gram_sum, cross_sum = lax.psum((gram_part, cross_part), ('cell', 'donor'))  253 us
    psum x1, waiting for transfers between devices, per_device(): gram_sum, cross_sum = lax.psum((gram_part, cross_part), ('cell', 'donor'))  193 us
    dot_general x49, matrix products, solve_written(): jnp.dot(factor[row + 1:, row], later, precision=lax.Precision.HIGHEST)  37.7 us
    dot_general x49, matrix products, solve_written(): jnp.dot(factor[row, :row], jnp.stack(forward), precision=lax.Precision.HI...  36.4 us
    reduce_sum x49, other arithmetic, factor_lower(): pivot = jnp.sqrt(gram_sum[column, column] - jnp.sum(known * known))  30 us
    scatter x50, local copies, waits for them, and re-layouts, factor_lower(): factor = factor.at[column + 1:, column].set(below / pivot)  19.3 us
    scatter x50, local copies, waits for them, and re-layouts, factor_lower(): factor = factor.at[column, column].set(pivot)  18.7 us
    another operation x1, loops' own time, association_block(): sliced = lax.map(one_gene, (gene_ids, starts))  16.7 us
  transfers between devices with their start and end apart: 3, of which 2 were waited for; matrix products, arithmetic and copies ran while one was open for 23% of the time, Pallas kernels for 0%

commit v1 on v0

--- a/solution.py
+++ b/solution.py
@@ -106,7 +106,7 @@
     design = with_intercept(covariates)
     gram_part = jnp.dot(design.T, design, precision=lax.Precision.HIGHEST)
     cross_part = jnp.einsum("dk,dcg->ckg", design, expression, precision=lax.Precision.HIGHEST)
-    gram_sum, cross_sum = lax.psum((gram_part, cross_part), ("cell", "donor"))
+    gram_sum, cross_sum = lax.psum(lax.psum((gram_part, cross_part), "donor"), "cell")
     coefficients = solve_normal(gram_sum, cross_sum)
     residual = expression - jnp.einsum(
         "dk,ckg->dcg", design, coefficients, precision=lax.Precision.HIGHEST

time: 824 us -> 572 us (0.69)
  blocking collectives: 267 us -> 67.7 us
  waiting for transfers between devices: 205 us -> 161 us
  local copies, waits for them, and re-layouts: 94.6 us -> 85.6 us
    psum x1 -> x2, blocking collectives: 253 us -> 53.6 us  [the longest x1 27 us: per_device(): lax.psum((gram_part, cross_part), 'donor')]
    psum x1 -> x2, waiting for transfers between devices: 193 us -> 149 us  [the longest x1 75.2 us: per_device(): lax.psum(lax.psum((gram_part, cross_part), 'donor'), 'cell')]
    dynamic_update_slice x8, local copies, waits for them, and re-layouts: 12.1 us -> 3.65 us  [association_block(): sliced = lax.map(one_gene, (gene_ids, starts))]
  transfers between devices with their start and end apart: 3 -> 4, of which waited for: 2 -> 3; matrix products, arithmetic and copies ran while one was open for 23% -> 33% of each run, Pallas kernels for 0% -> 0%
where the time goes in v1:
time: 572 us; the launch traced here: 561 us
  waiting for transfers between devices  161 us (28%)
  matrix products  95.7 us (17%)
  local copies, waits for them, and re-layouts  85.6 us (15%)
  between operations  83.7 us (15%)
  blocking collectives  67.7 us (12%)
  other arithmetic  38.9 us (7%)
  loops' own time  15.7 us (3%)
  starting transfers between devices  12.7 us (2%)
    psum x1, waiting for transfers between devices, per_device(): lax.psum(lax.psum((gram_part, cross_part), 'donor'), 'cell')  75.2 us
    psum x1, waiting for transfers between devices, per_device(): lax.psum((gram_part, cross_part), 'donor')  74.2 us
    dot_general x49, matrix products, solve_written(): jnp.dot(factor[row + 1:, row], later, precision=lax.Precision.HIGHEST)  37.4 us
    dot_general x49, matrix products, solve_written(): jnp.dot(factor[row, :row], jnp.stack(forward), precision=lax.Precision.HI...  36.2 us
    reduce_sum x49, other arithmetic, factor_lower(): pivot = jnp.sqrt(gram_sum[column, column] - jnp.sum(known * known))  30 us
    psum x1, blocking collectives, per_device(): lax.psum((gram_part, cross_part), 'donor')  27 us
    psum x1, blocking collectives, per_device(): lax.psum(lax.psum((gram_part, cross_part), 'donor'), 'cell')  26.6 us
    scatter x50, local copies, waits for them, and re-layouts, factor_lower(): factor = factor.at[column + 1:, column].set(below / pivot)  19.3 us
  transfers between devices with their start and end apart: 4, of which 3 were waited for; matrix products, arithmetic and copies ran while one was open for 33% of the time, Pallas kernels for 0%

profile of v1, /device:TPU:1, one launch (start us, length us, event | category | flops | bytes accessed | tf_op | source)
XLA Modules:
  0.0 561.2 jit_solution(1532693309045555996)
XLA Ops:
  7.3 2.8 fusion
  10.5 27.0 %psum.38 = f32[51,51]{1,0:T(8,128)S(1)} all-reduce(f32[51,51]{1,0:T(8,128)S(1)} %fusion.449), channel_id=1, replica_groups=mesh['cell'=8,'donor'=8,'gene'=8] {'donor'}, use_global_device_ids=true, to_apply=%region_5.6 | all-reduce | flops 2601 | bytes 20808 | tf_op jit(solution)/shard_map/psum | solution.py:109
  37.5 26.6 %psum.39 = f32[51,51]{1,0:T(8,128)S(1)} all-reduce(f32[51,51]{1,0:T(8,128)S(1)} %psum.38), channel_id=1, replica_groups=mesh['cell'=8,'donor'=8,'gene'=8] {'cell'}, use_global_device_ids=true, to_apply=%region_6.7 | all-reduce | flops 2601 | bytes 20808 | tf_op jit(solution)/shard_map/psum | solution.py:109
  176.8 11.7 %scatter.456 = f32[51,51]{1,0:T(8,128)S(1)} dynamic-update-slice(f32[51,51]{1,0:T(8,128)S(1)} %copy.363, f32[1,1]{1,0:T(1,128)} %bitcast.220, s32[]{:T(128)} %constant.2846.clone.1, s32[]{:T(128)} %constant.2846.clone.1) | dynamic-update-slice | bytes 12 | tf_op jit(solution)/shard_map/scatter | solution.py:25
  231.1 1.8 fusion.481
  270.5 0.8 fusion.250
  276.1 0.8 fusion.370
  296.7 0.8 fusion.293
  300.9 0.8 fusion.301
  311.4 1.0 reduce_sum.454
  312.5 14.1 %psum.35 = f32[192]{0:T(256)S(1)} all-reduce(f32[192]{0:T(256)S(1)} %reduce_sum.454), channel_id=1, replica_groups=mesh['cell'=8,'donor'=8,'gene'=8] {'gene'}, use_global_device_ids=true, to_apply=%region_2.3 | all-reduce | flops 192 | bytes 1536 | tf_op jit(solution)/shard_map/psum | solution.py:104
  326.5 1.0 log_multiply_fusion
  327.6 2.5 convolution_bitcast_fusion.1
  332.8 74.2 %all-reduce.6.cloned.1.call-done = f32[24,51,256]{2,1,0:T(8,128)} async-done(((f32[24,51,256]{2,1,0:T(8,128)}), f32[24,51,256]{2,1,0:T(8,128)}) %all-reduce.6.cloned.1.call-update) | async-done | bytes 1253392 | tf_op jit(solution)/shard_map/psum | solution.py:109
  412.2 1.4 fusion.335
  414.8 75.2 %all-reduce.8.cloned.1.call-done = f32[24,51,256]{2,1,0:T(8,128)} async-done(((f32[24,51,256]{2,1,0:T(8,128)}), f32[24,51,256]{2,1,0:T(8,128)}) %all-reduce.8.cloned.1.call-update) | async-done | bytes 1253392 | tf_op jit(solution)/shard_map/psum | solution.py:109
  490.0 2.6 convolution_bitcast_fusion
  493.8 1.5 reshape.3475
  495.3 12.4 %all-to-all-start = ((f32[64,1,768]{2,1,0:T(1,128)}), f32[64,1,768]{2,1,0:T(1,128)S(1)}, u32[]{:S(2)}, u32[]{:S(2)}) async-start(f32[64,1,768]{2,1,0:T(1,128)} %reshape.3475), calls=%async_computation.1 | async-start | bytes 393216 | tf_op jit(solution)/shard_map/all_to_all | solution.py:114
  507.9 11.7 %all-to-all-done = f32[64,1,768]{2,1,0:T(1,128)S(1)} async-done(((f32[64,1,768]{2,1,0:T(1,128)}), f32[64,1,768]{2,1,0:T(1,128)S(1)}, u32[]{:S(2)}, u32[]{:S(2)}) %all-to-all-start) | async-done | bytes 196640 | tf_op jit(solution)/shard_map/all_to_all | solution.py:114
  520.2 1.1 reduce.398
  522.2 6.6 %fusion.5 = f32[4,1024,24]{1,2,0:T(8,128)S(1)} fusion(s32[1024,512]{1,0:T(8,128)S(1)} %copy-done, f32[64,8,24,4]{2,1,3,0:T(8,128)S(1)} %bitcast.2482), kind=kOutput, calls=%fused_computation.9 | convolution fusion | flops 604504064 | bytes 2686976 | tf_op jit(solution)/shard_map/sd,dcg->gsc/dot_general | solution.py:63
  528.9 24.5 %while.115 = (s32[]{:T(128)}, f32[4,1024,24]{1,0,2:T(4,128)S(1)}, s32[4]{0:T(128)S(1)}, s32[4]{0:T(128)S(1)}, f32[4,2048,24]{1,2,0:T(8,128)S(1)}) while((s32[]{:T(128)}, f32[4,1024,24]{1,0,2:T(4,128)S(1)}, s32[4]{0:T(128)S(1)}, s32[4]{0:T(128)S(1)}, f32[4,2048,24]{1,2,0:T(8,128)S(1)}) %tuple.552), condition=%wide.region_57.58_spmd.clone, body=%wide.region_56.57_spmd.sunk.clone | while | flops 10 | bytes 590021 | solution.py:75
  553.4 0.9 multiply_bitcast_fusion
  (631 shorter events, 182.1 us)
Async XLA Ops:
  6.5 304.9 %reduce-scatter.2.cloned.1.call-start = ((), (), s32[]{:S(2)}) async-start(), calls=%async_computation.2 | async-start | bytes 1769472 | tf_op jit(solution)/shard_map/reduce_scatter | solution.py:98
  7.2 2.9 copy-start.2
  10.1 396.9 %all-reduce.6.cloned.1.call-start = ((), (), s32[]{:S(2)}) async-start(), calls=%async_computation.3 | async-start | bytes 2752512 | tf_op jit(solution)/shard_map/psum | solution.py:109
  330.1 159.9 %all-reduce.8.cloned.1.call-start = ((), (), s32[]{:S(2)}) async-start(), calls=%async_computation.4 | async-start | bytes 2752512 | tf_op jit(solution)/shard_map/psum | solution.py:109
  493.4 14.4 %copy-start.3 = (s32[4,1024]{1,0:T(4,128)S(1)}, s32[4,1024]{1,0:T(4,128)}, u32[]{:S(2)}) copy-start(s32[4,1024]{1,0:T(4,128)} %param.215) | copy-start | bytes 49156
  493.8 28.3 %copy-start = (s32[1024,512]{1,0:T(8,128)S(1)}, s32[1024,512]{1,0:T(8,128)}, u32[]{:S(2)}) copy-start(s32[1024,512]{1,0:T(8,128)} %param.214) | copy-start | bytes 6291460
  495.3 24.3 %all-to-all-start = ((f32[64,1,768]{2,1,0:T(1,128)}), f32[64,1,768]{2,1,0:T(1,128)S(1)}, u32[]{:S(2)}, u32[]{:S(2)}) async-start(f32[64,1,768]{2,1,0:T(1,128)} %reshape.3475), calls=%async_computation.1 | async-start | bytes 393216 | tf_op jit(solution)/shard_map/all_to_all | solution.py:114
  522.1 6.7 %copy-start.1 = (f32[4,1024,24]{1,0,2:T(4,128)S(1)}, f32[4,1024,24]{1,0,2:T(4,128)}, u32[]{:S(2)}) copy-start(f32[4,1024,24]{1,0,2:T(4,128)} %custom-call) | copy-start | bytes 1179652
Sparse Core Ops, SparseCore 0:
  10.3 45.5 reduce-scatter.1
  330.2 76.7 all-reduce.5
  409.5 80.4 all-reduce.7
